TPU v7x, 256 devices: a whole 4x4x8 slice. The times are simulated.
256 devices in a mesh: pairs: 64 (over z_hi, y, x), dates: 4 (over z_lo, core).
Axes of the slice: x: 4, y: 4, z: 8 (z_hi: 4, z_lo: 2; z = z_hi * 2 + z_lo), core: 2. Of those that a mesh axis runs over, the one named last changes fastest.
Arguments:
- returns: bfloat16 [4096, 32768], P('dates', 'pairs'), may hold values from -16 to 16
- plan: int32 [3, 64], P(None, 'pairs'), may hold values from 0 to 1
Outputs:
- rotated_panel: bfloat16 [4096, 32768], P('dates', 'pairs')
- disorder: float32 [3], replicated
All inputs are finite; a program needn't handle non-finite values.
Results may differ from a plain program's by a relative error of at most 0.0067.
Values may be sent and summed in bfloat16 or wider, within the bound.
A program may use at most 64 MiB of HBM per device.

v0:
```python
import jax
import jax.numpy as jnp
from jax import lax
from jax.sharding import PartitionSpec as P

B = 256
ROUNDS = 3
NS_STEPS = 3


damping_base = 0.5
epsilon = 1e-06


def shifted(x, axis, by):
    devices = lax.axis_size(axis)
    return lax.ppermute(x, axis, [(i, (i + by) % devices) for i in range(devices)])


def gathered_total(x, axis):
    pieces = lax.all_gather(x, axis).astype(jnp.float32)
    return pieces.sum(axis=0)


def from_everyone(x, axis):
    copies = jnp.broadcast_to(x, (lax.axis_size(axis), *x.shape))
    return lax.all_to_all(copies, axis, split_axis=0, concat_axis=0, tiled=True)


def over_copies(x, axis):
    everything = from_everyone(x, axis)
    return jnp.sum(everything, axis=0)


def gram_of(left, right):
    return lax.dot_general(
        left, right, (((0,), (0,)), ((), ())), preferred_element_type=jnp.float32
    )


def pass_on(block):
    return shifted(block, "pairs", 1)


def local(returns, plan):
    highest = lax.Precision.HIGHEST
    pairs_count = lax.axis_size("pairs")
    identity = jnp.eye(2 * B, dtype=jnp.float32)
    current = returns
    history = []
    for step_index in range(ROUNDS):
        left_part = current[:, :B]
        right_part = current[:, B:]
        left_left, left_right, right_right = (
            gathered_total(gram_of(left_part, left_part).astype(jnp.bfloat16), "dates").astype(
                jnp.float32
            ),
            gathered_total(gram_of(left_part, right_part).astype(jnp.bfloat16), "dates").astype(
                jnp.float32
            ),
            gathered_total(gram_of(right_part, right_part).astype(jnp.bfloat16), "dates").astype(
                jnp.float32
            ),
        )
        gram = jnp.concatenate(
            [
                jnp.concatenate([left_left, left_right], axis=1),
                jnp.concatenate([left_right.T, right_right], axis=1),
            ],
            axis=0,
        )
        diag_sum = jnp.diagonal(gram) + epsilon
        col_scale = jnp.sqrt(diag_sum)
        cross_block = gram[:B, B:] / (col_scale[:B, None] * col_scale[None, B:])
        coupling = jnp.sum(cross_block * cross_block)
        overall = over_copies(coupling / (B * B), "pairs")
        history.append(overall)
        damping = damping_base / jnp.sqrt(1.0 + B * B * overall / pairs_count)
        zeros_block = jnp.zeros_like(cross_block)
        skew_part = jnp.concatenate(
            [
                jnp.concatenate([zeros_block, -cross_block], axis=1),
                jnp.concatenate([cross_block.T, zeros_block], axis=1),
            ],
            axis=0,
        )
        factor = (identity + damping * skew_part) / jnp.sqrt(
            1.0 + 2.0 * damping * damping * coupling
        )
        for inner_step in range(NS_STEPS):
            squared = lax.dot_general(factor, factor, (((0,), (0,)), ((), ())), precision=highest)
            factor = 1.5 * factor - 0.5 * jnp.dot(factor, squared, precision=highest)
        rotation = factor.astype(jnp.bfloat16)
        chosen = plan[step_index, 0]
        moving_cols = jnp.where(chosen == 0, rotation[:, :B], rotation[:, B:])
        staying_cols = jnp.where(chosen == 0, rotation[:, B:], rotation[:, :B])
        outgoing = jnp.dot(current, moving_cols, preferred_element_type=jnp.float32).astype(
            jnp.bfloat16
        )
        incoming = pass_on(outgoing)
        staying = jnp.dot(current, staying_cols, preferred_element_type=jnp.float32).astype(
            jnp.bfloat16
        )
        current = jnp.where(
            chosen == 0,
            jnp.concatenate([incoming, staying], axis=1),
            jnp.concatenate([staying, incoming], axis=1),
        )
    return (current, jnp.stack(history))


def solution(mesh):
    return jax.shard_map(
        local,
        mesh=mesh,
        in_specs=(P("dates", "pairs"), P(None, "pairs")),
        out_specs=(P("dates", "pairs"), P()),
        check_vma=False,
    )
```

profile of v0, /device:TPU:32, one launch (start us, length us, event | category | flops | bytes accessed | tf_op | source)
XLA Modules:
  0.0 285.0 jit_solution(7308378013966651390)
XLA Ops:
  0.7 1.6 convolution_convert_fusion.12
  2.3 0.3 convolution_convert_fusion.14
  2.7 0.3 convolution_convert_fusion.13
  3.0 7.5 %all-gather.1 = bf16[1024,256]{1,0:T(8,128)(2,1)S(1)} all-gather(bf16[256,256]{1,0:T(8,128)(2,1)S(1)} %convolution_convert_fusion.13), channel_id=3, replica_groups=mesh['pairs'=64,'dates'=4] {'dates'}, dimensions={0}, use_global_device_ids=true | all-gather | bytes 655360 | tf_op jit(solution)/shard_map/all_gather | solution.py:21
  10.6 7.3 %all-gather = bf16[1024,256]{1,0:T(8,128)(2,1)S(1)} all-gather(bf16[256,256]{1,0:T(8,128)(2,1)S(1)} %convolution_convert_fusion.14), channel_id=2, replica_groups=mesh['pairs'=64,'dates'=4] {'dates'}, dimensions={0}, use_global_device_ids=true | all-gather | bytes 655360 | tf_op jit(solution)/shard_map/all_gather | solution.py:21
  18.1 7.3 %all-gather.2 = bf16[1024,256]{1,0:T(8,128)(2,1)S(1)} all-gather(bf16[256,256]{1,0:T(8,128)(2,1)S(1)} %convolution_convert_fusion.12), channel_id=4, replica_groups=mesh['pairs'=64,'dates'=4] {'dates'}, dimensions={0}, use_global_device_ids=true | all-gather | bytes 655360 | tf_op jit(solution)/shard_map/all_gather | solution.py:21
  25.6 4.5 %gather_fusion = f32[512]{0:T(512)S(1)} fusion(f32[512,512]{1,0:T(8,128)S(1)} %maximum_maximum_fusion, s32[512]{0:T(512)S(1)} %bitcast.68), kind=kCustom, calls=%fused_computation | custom fusion | bytes 8192 | tf_op jit(solution)/shard_map/jit(diagonal)/cond/branch_0_fun/gather | solution.py:72
  30.2 0.8 multiply_reduce_fusion.2
  31.6 0.6 broadcast_in_dim.23
  32.2 13.1 %all-to-all-start = ((f32[64,1,1]{2,1,0:T(1,128)}), f32[64,1,1]{2,1,0:T(1,128)S(1)}, u32[]{:S(2)}, u32[]{:S(2)}) async-start(f32[64,1,1]{2,1,0:T(1,128)} %broadcast_in_dim.23), calls=%async_computation | async-start | bytes 65536 | tf_op jit(solution)/shard_map/all_to_all | solution.py:27
  45.4 0.6 fusion.89
  46.7 10.6 %all-to-all-done = f32[64,1,1]{2,1,0:T(1,128)S(1)} async-done(((f32[64,1,1]{2,1,0:T(1,128)}), f32[64,1,1]{2,1,0:T(1,128)S(1)}, u32[]{:S(2)}, u32[]{:S(2)}) %all-to-all-start) | async-done | bytes 288 | tf_op jit(solution)/shard_map/all_to_all | solution.py:27
  57.3 0.7 reduce_sum.139
  59.4 1.9 fusion.62
  61.3 1.9 fusion.8
  63.3 1.9 fusion.90
  65.1 1.9 fusion.7
  67.0 1.9 fusion.91
  69.0 1.9 fusion.9
  70.9 0.5 fusion.12
  71.4 1.1 collective-permute-start
  72.5 0.5 fusion.13
  73.0 29.2 %collective-permute-done = bf16[1024,256]{0,1:T(8,128)(2,1)S(1)} collective-permute-done((bf16[1024,256]{0,1:T(8,128)(2,1)S(1)}, bf16[1024,256]{0,1:T(8,128)(2,1)S(1)}, u32[]{:S(2)}, u32[]{:S(2)}) %collective-permute-start) | collective-permute-done | bytes 524320 | tf_op jit(solution)/shard_map/ppermute | solution.py:17
  102.2 0.5 maximum_select_fusion
  103.7 6.5 %all-gather.4 = bf16[1024,256]{1,0:T(8,128)(2,1)S(1)} all-gather(bf16[256,256]{1,0:T(8,128)(2,1)S(1)} %convolution_convert_fusion.10), channel_id=6, replica_groups=mesh['pairs'=64,'dates'=4] {'dates'}, dimensions={0}, use_global_device_ids=true | all-gather | bytes 655360 | tf_op jit(solution)/shard_map/all_gather | solution.py:21
  110.3 7.3 %all-gather.3 = bf16[1024,256]{1,0:T(8,128)(2,1)S(1)} all-gather(bf16[256,256]{1,0:T(8,128)(2,1)S(1)} %convolution_convert_fusion.11), channel_id=5, replica_groups=mesh['pairs'=64,'dates'=4] {'dates'}, dimensions={0}, use_global_device_ids=true | all-gather | bytes 655360 | tf_op jit(solution)/shard_map/all_gather | solution.py:21
  117.8 7.3 %all-gather.5 = bf16[1024,256]{1,0:T(8,128)(2,1)S(1)} all-gather(bf16[256,256]{1,0:T(8,128)(2,1)S(1)} %convolution_convert_fusion.9), channel_id=7, replica_groups=mesh['pairs'=64,'dates'=4] {'dates'}, dimensions={0}, use_global_device_ids=true | all-gather | bytes 655360 | tf_op jit(solution)/shard_map/all_gather | solution.py:21
  125.3 4.5 %gather_fusion.1 = f32[512]{0:T(512)S(1)} fusion(f32[512,512]{1,0:T(8,128)S(1)} %maximum_maximum_fusion.1, s32[512]{0:T(512)S(1)} %bitcast.69), kind=kCustom, calls=%fused_computation.1 | custom fusion | bytes 8192 | tf_op jit(solution)/shard_map/jit(diagonal)/cond/branch_0_fun/gather | solution.py:72
  129.9 0.8 multiply_reduce_fusion.1
  131.4 0.6 broadcast_in_dim.24
  132.0 4.6 %all-to-all-start.1 = ((f32[64,1,1]{2,1,0:T(1,128)}), f32[64,1,1]{2,1,0:T(1,128)S(1)}, u32[]{:S(2)}, u32[]{:S(2)}) async-start(f32[64,1,1]{2,1,0:T(1,128)} %broadcast_in_dim.24), calls=%async_computation.1 | async-start | bytes 65536 | tf_op jit(solution)/shard_map/all_to_all | solution.py:27
  137.1 11.2 %all-to-all-done.1 = f32[64,1,1]{2,1,0:T(1,128)S(1)} async-done(((f32[64,1,1]{2,1,0:T(1,128)}), f32[64,1,1]{2,1,0:T(1,128)S(1)}, u32[]{:S(2)}, u32[]{:S(2)}) %all-to-all-start.1) | async-done | bytes 288 | tf_op jit(solution)/shard_map/all_to_all | solution.py:27
  148.4 0.7 reduce_sum.144
  150.3 1.9 fusion.59
  152.2 1.9 fusion.5
  154.1 1.9 fusion.92
  156.0 1.9 fusion.4
  157.9 1.9 fusion.93
  159.8 1.9 fusion.10
  161.8 0.5 convolution_convert_fusion.3
  162.3 0.8 collective-permute-start.1
  163.1 0.5 convolution_convert_fusion.2
  163.6 29.5 %collective-permute-done.1 = bf16[1024,256]{1,0:T(8,128)(2,1)S(1)} collective-permute-done((bf16[1024,256]{1,0:T(8,128)(2,1)S(1)}, bf16[1024,256]{1,0:T(8,128)(2,1)S(1)}, u32[]{:S(2)}, u32[]{:S(2)}) %collective-permute-start.1) | collective-permute-done | bytes 524320 | tf_op jit(solution)/shard_map/ppermute | solution.py:17
  194.4 6.5 %all-gather.7 = bf16[1024,256]{1,0:T(8,128)(2,1)S(1)} all-gather(bf16[256,256]{1,0:T(8,128)(2,1)S(1)} %convolution_convert_fusion.7), channel_id=9, replica_groups=mesh['pairs'=64,'dates'=4] {'dates'}, dimensions={0}, use_global_device_ids=true | all-gather | bytes 655360 | tf_op jit(solution)/shard_map/all_gather | solution.py:21
  201.0 7.3 %all-gather.6 = bf16[1024,256]{1,0:T(8,128)(2,1)S(1)} all-gather(bf16[256,256]{1,0:T(8,128)(2,1)S(1)} %convolution_convert_fusion.8), channel_id=8, replica_groups=mesh['pairs'=64,'dates'=4] {'dates'}, dimensions={0}, use_global_device_ids=true | all-gather | bytes 655360 | tf_op jit(solution)/shard_map/all_gather | solution.py:21
  208.5 7.3 %all-gather.8 = bf16[1024,256]{1,0:T(8,128)(2,1)S(1)} all-gather(bf16[256,256]{1,0:T(8,128)(2,1)S(1)} %convolution_convert_fusion.6), channel_id=10, replica_groups=mesh['pairs'=64,'dates'=4] {'dates'}, dimensions={0}, use_global_device_ids=true | all-gather | bytes 655360 | tf_op jit(solution)/shard_map/all_gather | solution.py:21
  216.0 4.5 %gather_fusion.2 = f32[512]{0:T(512)S(1)} fusion(f32[512,512]{1,0:T(8,128)S(1)} %maximum_maximum_fusion.2, s32[512]{0:T(512)S(1)} %bitcast.70), kind=kCustom, calls=%fused_computation.2 | custom fusion | bytes 8192 | tf_op jit(solution)/shard_map/jit(diagonal)/cond/branch_0_fun/gather | solution.py:72
  220.6 0.8 multiply_reduce_fusion
  222.0 0.6 broadcast_in_dim.25
  222.7 4.6 %all-to-all-start.2 = ((f32[64,1,1]{2,1,0:T(1,128)}), f32[64,1,1]{2,1,0:T(1,128)S(1)}, u32[]{:S(2)}, u32[]{:S(2)}) async-start(f32[64,1,1]{2,1,0:T(1,128)} %broadcast_in_dim.25), calls=%async_computation.2 | async-start | bytes 65536 | tf_op jit(solution)/shard_map/all_to_all | solution.py:27
  227.9 11.1 %all-to-all-done.2 = f32[64,1,1]{2,1,0:T(1,128)S(1)} async-done(((f32[64,1,1]{2,1,0:T(1,128)}), f32[64,1,1]{2,1,0:T(1,128)S(1)}, u32[]{:S(2)}, u32[]{:S(2)}) %all-to-all-start.2) | async-done | bytes 288 | tf_op jit(solution)/shard_map/all_to_all | solution.py:27
  239.0 0.7 reduce_sum.149
  241.1 1.9 fusion.56
  243.0 1.9 fusion.2
  244.9 1.9 fusion.94
  246.8 1.9 fusion.1
  248.7 1.9 fusion.95
  250.6 1.9 fusion.11
  252.5 0.4 convolution_convert_fusion.1
  253.0 0.6 collective-permute-start.2
  253.6 2.5 pad_maximum_fusion
  256.1 0.4 convolution_convert_fusion
  256.5 27.1 %collective-permute-done.2 = bf16[1024,256]{1,0:T(8,128)(2,1)S(1)} collective-permute-done((bf16[1024,256]{1,0:T(8,128)(2,1)S(1)}, bf16[1024,256]{1,0:T(8,128)(2,1)S(1)}, u32[]{:S(2)}, u32[]{:S(2)}) %collective-permute-start.2) | collective-permute-done | bytes 524320 | tf_op jit(solution)/shard_map/ppermute | solution.py:17
  283.6 1.2 maximum_select_fusion.2
  (33 shorter events, 3.8 us)
Async XLA Ops:
  0.6 1.7 copy-start.1
  30.1 15.2 %copy-start = (s32[3,1]{0,1:T(1,128)S(1)}, s32[3,1]{0,1:T(1,128)}, u32[]{:S(2)}) copy-start(s32[3,1]{0,1:T(1,128)} %param.3) | copy-start | bytes 40
  32.2 25.0 %all-to-all-start = ((f32[64,1,1]{2,1,0:T(1,128)}), f32[64,1,1]{2,1,0:T(1,128)S(1)}, u32[]{:S(2)}, u32[]{:S(2)}) async-start(f32[64,1,1]{2,1,0:T(1,128)} %broadcast_in_dim.23), calls=%async_computation | async-start | bytes 65536 | tf_op jit(solution)/shard_map/all_to_all | solution.py:27
  71.4 30.9 %collective-permute-start = (bf16[1024,256]{0,1:T(8,128)(2,1)S(1)}, bf16[1024,256]{0,1:T(8,128)(2,1)S(1)}, u32[]{:S(2)}, u32[]{:S(2)}) collective-permute-start(bf16[1024,256]{0,1:T(8,128)(2,1)S(1)} %fusion.12), channel_id=1, source_target_pairs={{0,4},{4,8},{8,12},{12,16},{16,20},{20,24},{24,28},{28,32},{32,36}... | collective-permute-start | bytes 1572872 | tf_op jit(solution)/shard_map/ppermute | solution.py:17
  132.0 16.4 %all-to-all-start.1 = ((f32[64,1,1]{2,1,0:T(1,128)}), f32[64,1,1]{2,1,0:T(1,128)S(1)}, u32[]{:S(2)}, u32[]{:S(2)}) async-start(f32[64,1,1]{2,1,0:T(1,128)} %broadcast_in_dim.24), calls=%async_computation.1 | async-start | bytes 65536 | tf_op jit(solution)/shard_map/all_to_all | solution.py:27
  162.3 30.8 %collective-permute-start.1 = (bf16[1024,256]{1,0:T(8,128)(2,1)S(1)}, bf16[1024,256]{1,0:T(8,128)(2,1)S(1)}, u32[]{:S(2)}, u32[]{:S(2)}) collective-permute-start(bf16[1024,256]{1,0:T(8,128)(2,1)S(1)} %convolution_convert_fusion.3), channel_id=1, source_target_pairs={{0,4},{4,8},{8,12},{12,16},{16,20},{20,24},{24,28},{28,32},{32,36}... | collective-permute-start | bytes 1572872 | tf_op jit(solution)/shard_map/ppermute | solution.py:17
  222.7 16.4 %all-to-all-start.2 = ((f32[64,1,1]{2,1,0:T(1,128)}), f32[64,1,1]{2,1,0:T(1,128)S(1)}, u32[]{:S(2)}, u32[]{:S(2)}) async-start(f32[64,1,1]{2,1,0:T(1,128)} %broadcast_in_dim.25), calls=%async_computation.2 | async-start | bytes 65536 | tf_op jit(solution)/shard_map/all_to_all | solution.py:27
  253.0 30.7 %collective-permute-start.2 = (bf16[1024,256]{1,0:T(8,128)(2,1)S(1)}, bf16[1024,256]{1,0:T(8,128)(2,1)S(1)}, u32[]{:S(2)}, u32[]{:S(2)}) collective-permute-start(bf16[1024,256]{1,0:T(8,128)(2,1)S(1)} %convolution_convert_fusion.1), channel_id=1, source_target_pairs={{0,4},{4,8},{8,12},{12,16},{16,20},{20,24},{24,28},{28,32},{32,36}... | collective-permute-start | bytes 1572872 | tf_op jit(solution)/shard_map/ppermute | solution.py:17
where the time goes:
time: 288 us; the launch traced here: 285 us
  waiting for transfers between devices  119 us (41%)
  blocking collectives  64.3 us (22%)
  matrix products  41.4 us (14%)
  starting transfers between devices  24.9 us (9%)
  local copies, waits for them, and re-layouts  16.5 us (6%)
  other arithmetic  10 us (3%)
  between operations  9.17 us (3%)
    ppermute x3, waiting for transfers between devices, shifted(): lax.ppermute(x, axis, [(i, (i + by) % devices) for i in range(devices)])  85.8 us
    all_gather x9, blocking collectives, gathered_total(): pieces = lax.all_gather(x, axis).astype(jnp.float32)  64.3 us
    all_to_all x3, waiting for transfers between devices, from_everyone(): return lax.all_to_all(copies, axis, split_axis=0, concat_axis=0, tiled=True)  32.9 us
    all_to_all x3, starting transfers between devices, from_everyone(): return lax.all_to_all(copies, axis, split_axis=0, concat_axis=0, tiled=True)  22.3 us
    dot_general x9, matrix products, local(): factor = 1.5 * factor - 0.5 * jnp.dot(factor, squared, precision=highest)  17.2 us
    dot_general x9, matrix products, local(): lax.dot_general(factor, factor, (((0,), (0,)), ((), ())), precision=highest)  17 us
    gather x3, local copies, waits for them, and re-layouts, local(): diag_sum = jnp.diagonal(gram) + epsilon  13.6 us
  transfers between devices with their start and end apart: 6, of which 6 were waited for; matrix products, arithmetic and copies ran while one was open for 2% of the time, Pallas kernels for 0%

commit v1 on v0

v1 whole, which is shorter than its diff:
```python
import functools

import jax
import jax.numpy as jnp
from jax import lax
from jax.experimental import pallas as pl
from jax.experimental.pallas import tpu as pltpu
from jax.sharding import PartitionSpec as P

ROUNDS = 3
damping_base = 0.5
epsilon = 1e-06
MESH = pl.DeviceIdType.MESH
F32 = jnp.float32
BF16 = jnp.bfloat16
PIECES = 4
RELAYED = (2, 3)


def mm(a, b):
    return jnp.dot(a.astype(BF16), b.astype(BF16), preferred_element_type=F32)


def mm_tn(a, b):
    return lax.dot_general(a, b, (((0,), (0,)), ((), ())), preferred_element_type=F32)


def send(src, dst, send_sem, recv_sem, device):
    return pltpu.make_async_remote_copy(
        src_ref=src, dst_ref=dst, send_sem=send_sem, recv_sem=recv_sem, device_id=device, device_id_type=MESH
    )


def steps_between(k, n_pairs, row):
    x, y, z = k % row, (k // row) % row, k // (row * row)
    depth = n_pairs // (row * row)
    return min(x, row - x) + min(y, row - y) + 2 * min(z, depth - z)


class Side:
    def __init__(self, m):
        self.m = m
        self.m2 = mm(m, m)
        self.m3 = mm(self.m2, m)

    def finish(self, n, t):
        w = 1.5 - 0.5 * n
        tau = n * w * w
        e = t * (w * w - n * w) * self.m + t * t * (0.25 * n - w) * self.m2 + (0.25 * t * t * t) * self.m3
        w1 = 1.5 - 0.5 * tau
        e2 = mm(e, e)
        y = t * self.m
        self.gb = (-0.5 * w) * e - (0.5 * w1) * y + 0.25 * mm(y, e)
        self.hb = w * w1
        e3 = mm(e, e2)
        self.f = -0.5 * ((w1 * w1 - tau * w1) * e + (0.25 * tau - w1) * e2 + 0.25 * e3)
        self.w2 = 1.5 - 0.5 * tau * w1 * w1
        self.h = self.hb * self.w2
        self.hn = self.hb * self.f + self.w2 * self.gb + mm(self.gb, self.f)

    def right_of(self, d):
        r = self.hb * d + mm(d, self.gb)
        return self.w2 * r + mm(r, self.f)


def kernel(n_pairs, n_dates, x_ref, plan_ref, inc_out, stay_out, dis_ref,
           inc_buf, mov_buf, relay_buf, stay_buf, pan, gram_buf, share, shares,
           ring_send, ring_recv, relay_send, relay_recv, fwd_send, gram_send, gram_recv, share_send, share_recv):
    rows, b2 = x_ref.shape
    b = b2 // 2
    half = b // 2
    height = rows // PIECES
    plane = n_pairs // 4
    p, d = lax.axis_index("pairs"), lax.axis_index("dates")
    following = lax.rem(p + 1, n_pairs)

    barrier = pltpu.get_barrier_semaphore()
    for k in range(1, n_pairs):
        pl.semaphore_signal(barrier, inc=1, device_id=(lax.rem(p + k, n_pairs), d), device_id_type=MESH)
    for k in range(1, n_dates):
        pl.semaphore_signal(barrier, inc=1, device_id=(p, lax.rem(d + k, n_dates)), device_id_type=MESH)

    is_corner = lax.rem(p, plane) == plane - 1
    is_relay = lax.rem(p, plane) == 0
    relay_at = lax.rem(p - (plane - 1) + n_pairs, n_pairs)
    relay_to = lax.rem(p + plane, n_pairs)

    eye_half = lax.broadcasted_iota(jnp.int32, (half, half), 0) == lax.broadcasted_iota(jnp.int32, (half, half), 1)
    eye = (lax.broadcasted_iota(jnp.int32, (b, b), 0) == lax.broadcasted_iota(jnp.int32, (b, b), 1)).astype(F32)
    extra_row = lax.broadcasted_iota(jnp.int32, (16, b), 0)
    order = sorted(range(1, n_pairs), key=lambda k: -steps_between(k, n_pairs, 4))
    pieces = [(c, i) for c in range(2) for i in range(PIECES)]
    relayed = [(c, i) for c in range(2) for i in RELAYED]

    def split(v):
        hi = v.astype(BF16).astype(F32)
        return hi, v - hi

    previous_slot = None
    for r in range(ROUNDS):
        slot = plan_ref[r, 0]
        if r == 0:
            moves_inc = slot == 0
            inc = [x_ref.at[:, pl.ds(half * c, half)] for c in range(2)]
            stay = x_ref.at[:, pl.ds(b, b)]
        else:
            moves_inc = slot == previous_slot
            inc = [inc_buf.at[r - 1, c] for c in range(2)]
            stay = stay_buf.at[r - 1]
        previous_slot = slot
        sign = jnp.where(slot == 0, 1.0, -1.0).astype(F32)

        stay_f32 = stay[...].astype(F32)
        stay_sq = jnp.sum(stay_f32 * stay_f32, axis=0, keepdims=True)
        stay_hi, stay_lo = split(stay_sq)
        gram_copies = []
        for c in range(2):
            if r > 0:
                for i in range(PIECES):
                    incoming[c, i].wait_recv()
            inc_f32 = inc[c][...].astype(F32)
            inc_hi, inc_lo = split(jnp.sum(inc_f32 * inc_f32, axis=0, keepdims=True))
            mine = gram_buf.at[r, c, d]
            mine[0:half, :] = mm_tn(inc[c][...], stay[...]).astype(BF16)
            extra = jnp.where(extra_row == 0, jnp.concatenate([inc_hi, inc_lo], axis=1), 0.0)
            extra = jnp.where(extra_row == 1, stay_hi, extra)
            extra = jnp.where(extra_row == 2, stay_lo, extra)
            mine[half:half + 16, :] = extra.astype(BF16)
            if r == 0 and c == 0:
                pl.semaphore_wait(barrier, n_pairs - 1 + n_dates - 1)
            for k in range(1, n_dates):
                copy = send(mine, mine, gram_send.at[r, c, k - 1], gram_recv.at[r, c, k - 1], (p, lax.rem(d + k, n_dates)))
                copy.start()
                gram_copies.append(copy)
            if r > 0 and c == 0:
                forward(1)
        cross = []
        for c in range(2):
            for k in range(n_dates - 1):
                gram_copies[c * (n_dates - 1) + k].wait_recv()
            total = gram_buf[r, c, 0].astype(F32)
            for k in range(1, n_dates):
                total = total + gram_buf[r, c, k].astype(F32)
            inc_scale = lax.rsqrt(total[half:half + 1, :half] + total[half:half + 1, half:] + epsilon)
            stay_scale = lax.rsqrt(total[half + 1:half + 2] + total[half + 2:half + 3] + epsilon)
            inc_scale = jnp.sum(jnp.where(eye_half, inc_scale, 0.0), axis=1, keepdims=True)
            cross.append(total[0:half] * inc_scale * stay_scale)
        cross = jnp.concatenate(cross, axis=0)
        coupling = jnp.sum(jnp.sum(cross * cross, axis=0, keepdims=True), axis=1, keepdims=True)

        mine = jnp.broadcast_to(coupling * (1.0 / (b * b)), (8, 128))
        share[r] = mine
        shares[r, pl.ds(p, 1), :] = mine[0:1]
        share_copies = []
        for k in order:
            copy = send(share.at[r, pl.ds(0, 1)], shares.at[r, pl.ds(p, 1)], share_send.at[r], share_recv.at[r],
                        (lax.rem(p + k, n_pairs), d))
            copy.start()
            share_copies.append(copy)

        cross_t = cross.T
        d_mov = lax.select(moves_inc, cross, cross_t)
        d_mov_t = lax.select(moves_inc, cross_t, cross)
        mov_side = Side(mm(d_mov, d_mov_t))
        stay_side = Side(mm(d_mov_t, d_mov))
        for c in range(2):
            one, two = inc[c][...], stay[:, half * c:half * (c + 1)]
            pan[:, half * c:half * (c + 1)] = lax.select(moves_inc, one, two)
            pan[:, b + half * c:b + half * (c + 1)] = lax.select(moves_inc, two, one)

        everyone = send(shares.at[r, pl.ds(0, n_pairs - 1)], shares.at[r, pl.ds(0, n_pairs - 1)], share_send.at[r],
                        share_recv.at[r], (following, d))
        everyone.wait_recv()
        overall = jnp.sum(shares[r], axis=0, keepdims=True)
        dis_ref[r:r + 1, :] = overall
        overall = overall[:, 0:1]
        damping = damping_base / jnp.sqrt(1.0 + float(b * b) * overall / n_pairs)
        n = 1.0 / (1.0 + 2.0 * damping * damping * coupling)
        t = n * damping * damping
        a = jnp.sqrt(n)
        ad = a * damping * sign

        mov_side.finish(n, t)
        top = a * mov_side.h * eye + a * mov_side.hn
        bottom = ad * mov_side.right_of(d_mov_t)
        rotation = jnp.concatenate([top, bottom], axis=0).astype(BF16)

        landing = inc_out if r == ROUNDS - 1 else inc_buf.at[r]
        incoming, by_relay, forwards = {}, {}, {}
        for q, (c, i) in enumerate(pieces):
            place = pl.ds(height * i, height)
            incoming[c, i] = send(mov_buf.at[r, c, place], landing.at[c, place], ring_send.at[r, q], ring_recv.at[r, q], (following, d))
        for q, (c, i) in enumerate(relayed):
            place = pl.ds(height * i, height)
            way = relay_buf.at[r, q]
            by_relay[c, i] = send(mov_buf.at[r, c, place], way, relay_send.at[r, q], relay_recv.at[r, q], (relay_at, d))
            forwards[c, i] = send(way, landing.at[c, place], fwd_send.at[r, q], ring_recv.at[r, c * PIECES + i], (relay_to, d))

        def pass_on(c, i, incoming=incoming, by_relay=by_relay):
            if i in RELAYED:
                @pl.when(is_corner)
                def _():
                    by_relay[c, i].start()

                @pl.when(jnp.logical_not(is_corner))
                def _():
                    incoming[c, i].start()
            else:
                incoming[c, i].start()

        def forward(c, by_relay=by_relay, forwards=forwards):
            @pl.when(is_relay)
            def _():
                for i in RELAYED:
                    by_relay[c, i].wait_recv()
                    forwards[c, i].start()

        for i in range(PIECES):
            place = pl.ds(height * i, height)
            part = jnp.dot(pan[place, :], rotation, preferred_element_type=F32).astype(BF16)
            mov_buf[r, 0, place, :] = part[:, :half]
            mov_buf[r, 1, place, :] = part[:, half:]
            pass_on(0, i)
        for i in range(PIECES):
            pass_on(1, i)

        stay_side.finish(n, t)
        top = (-ad) * stay_side.right_of(d_mov)
        bottom = a * stay_side.h * eye + a * stay_side.hn
        rotation = jnp.concatenate([top, bottom], axis=0).astype(BF16)
        target = stay_out if r == ROUNDS - 1 else stay_buf.at[r]
        target[...] = jnp.dot(pan[...], rotation, preferred_element_type=F32).astype(BF16)
        forward(0)

        for copy in gram_copies:
            copy.wait_send()
        everyone.wait_send()
        if r == ROUNDS - 1:
            forward(1)
            for c, i in pieces:
                incoming[c, i].wait_recv()
        def finish(incoming=incoming, by_relay=by_relay, forwards=forwards):
            for c, i in pieces:
                if i in RELAYED:
                    @pl.when(is_corner)
                    def _():
                        by_relay[c, i].wait_send()

                    @pl.when(jnp.logical_not(is_corner))
                    def _():
                        incoming[c, i].wait_send()
                else:
                    incoming[c, i].wait_send()

            @pl.when(is_relay)
            def _():
                for k in relayed:
                    forwards[k].wait_send()
        finishes = [finish] if r == 0 else finishes + [finish]
    for finish in finishes:
        finish()


def local(n_pairs, n_dates, returns, plan):
    rows, b2 = returns.shape
    b = b2 // 2
    half = b // 2
    height = rows // PIECES
    dma = pltpu.SemaphoreType.DMA
    vmem = pl.BlockSpec(memory_space=pltpu.VMEM)
    moved, stayed, disorder = pl.pallas_call(
        functools.partial(kernel, n_pairs, n_dates),
        out_shape=(
            jax.ShapeDtypeStruct((2, rows, half), BF16),
            jax.ShapeDtypeStruct((rows, b), BF16),
            jax.ShapeDtypeStruct((8, 128), F32),
        ),
        in_specs=[vmem, pl.BlockSpec(memory_space=pltpu.SMEM)],
        out_specs=(vmem, vmem, vmem),
        scratch_shapes=[
            pltpu.VMEM((ROUNDS - 1, 2, rows, half), BF16),
            pltpu.VMEM((ROUNDS, 2, rows, half), BF16),
            pltpu.VMEM((ROUNDS, 2 * len(RELAYED), height, half), BF16),
            pltpu.VMEM((ROUNDS - 1, rows, b), BF16),
            pltpu.VMEM((rows, b2), BF16),
            pltpu.VMEM((ROUNDS, 2, n_dates, half + 16, b), BF16),
            pltpu.VMEM((ROUNDS, 8, 128), F32),
            pltpu.VMEM((ROUNDS, n_pairs, 128), F32),
            dma((ROUNDS, 2 * PIECES)),
            dma((ROUNDS, 2 * PIECES)),
            dma((ROUNDS, 2 * len(RELAYED))),
            dma((ROUNDS, 2 * len(RELAYED))),
            dma((ROUNDS, 2 * len(RELAYED))),
            dma((ROUNDS, 2, n_dates - 1)),
            dma((ROUNDS, 2, n_dates - 1)),
            dma((ROUNDS,)),
            dma((ROUNDS,)),
        ],
        compiler_params=pltpu.CompilerParams(collective_id=0, has_side_effects=True, vmem_limit_bytes=48 << 20),
        name="jacobi_rounds",
    )(returns, plan)
    front = jnp.concatenate([moved[0], moved[1], stayed], axis=1)
    back = jnp.concatenate([stayed, moved[0], moved[1]], axis=1)
    return jnp.where(plan[ROUNDS - 1, 0] == 0, front, back), disorder[:ROUNDS, 0]


def solution(mesh):
    return jax.shard_map(
        functools.partial(local, mesh.shape["pairs"], mesh.shape["dates"]),
        mesh=mesh,
        in_specs=(P("dates", "pairs"), P(None, "pairs")),
        out_specs=(P("dates", "pairs"), P()),
        check_vma=False,
    )
```

time: 288 us -> 132 us (0.46)
  Pallas kernels: 0 us -> 125 us
  waiting for transfers between devices: 119 us -> 0 us
  blocking collectives: 64.3 us -> 0 us
  matrix products: 41.4 us -> 0 us
  starting transfers between devices: 24.9 us -> 0 us
  local copies, waits for them, and re-layouts: 16.5 us -> 3.87 us
  other arithmetic: 10 us -> 1.35 us
  between operations: 9.17 us -> 1.3 us
    pallas_call x0 -> x1, Pallas kernels: none -> 125 us  [local(): pl.pallas_call(functools.partial(kernel, n_pairs, n_dates), out_shape=(ja...]
    ppermute x3 -> x0, waiting for transfers between devices: 85.8 us -> none  [shifted(): lax.ppermute(x, axis, [(i, (i + by) % devices) for i in range(devices)])]
    all_gather x9 -> x0, blocking collectives: 64.3 us -> none  [gathered_total(): pieces = lax.all_gather(x, axis).astype(jnp.float32)]
    dot_general x33 -> x0, matrix products: 41.4 us -> none  [the longest x9 17.2 us: local(): factor = 1.5 * factor - 0.5 * jnp.dot(factor, squared, precision=highest)]
    all_to_all x3 -> x0, waiting for transfers between devices: 32.9 us -> none  [from_everyone(): return lax.all_to_all(copies, axis, split_axis=0, concat_axis=0, tiled=True)]
    all_to_all x3 -> x0, starting transfers between devices: 22.3 us -> none  [from_everyone(): return lax.all_to_all(copies, axis, split_axis=0, concat_axis=0, tiled=True)]
    gather x3 -> x0, local copies, waits for them, and re-layouts: 13.6 us -> none  [local(): diag_sum = jnp.diagonal(gram) + epsilon]
    reduce_sum x15 -> x0, other arithmetic: 5.1 us -> none  [the longest x3 2.41 us: local(): coupling = jnp.sum(cross_block * cross_block)]
  transfers between devices with their start and end apart: 6 -> 0, of which waited for: 6 -> 0; matrix products, arithmetic and copies ran while one was open for 2% -> 0% of each run, Pallas kernels for 0% -> 0%
where the time goes in v1:
time: 132 us
  Pallas kernels  125 us (95%)
  local copies, waits for them, and re-layouts  3.87 us (3%)
  other arithmetic  1.35 us (1%)
    pallas_call x1, Pallas kernels, local(): pl.pallas_call(functools.partial(kernel, n_pairs, n_dates), out_shape=(ja...  125 us

profile of v1, /device:TPU:32, one launch (start us, length us, event | category | flops | bytes accessed | tf_op | source)
XLA Modules:
  0.0 131.8 jit_solution(12726291366367678454)
XLA Ops:
  0.6 1.2 slice.14
  2.5 0.7 copy.5.plan_ref
  3.3 0.0 copy-start
  3.3 1.2 copy-done
  4.5 125.3 %jacobi_rounds.1 = (bf16[2,1024,128]{2,1,0:T(8,128)(2,1)S(1)}, bf16[1024,256]{1,0:T(8,128)(2,1)S(1)}, f32[8,128]{1,0:T(8,128)S(1)}) custom-call(bf16[1024,512]{1,0:T(8,128)(2,1)S(1)} %copy-done, s32[3,1]{1,0:T(4,128)S(1)} %copy.5.plan_ref), custom_call_target="tpu_custom_call" | custom-call | tf_op jit(solution)/shard_map/jacobi_rounds/pallas_call | solution.py:271
  129.8 1.3 %maximum_select_fusion = bf16[1024,512]{1,0:T(8,128)(2,1)} fusion(bf16[1024,256]{1,0:T(8,128)(2,1)S(1)} %get-tuple-element.6, bf16[1024,128]{1,0:T(8,128)(2,1)S(1)} %get-tuple-element.9, bf16[1024,128]{1,0:T(8,128)(2,1)S(1)} %get-tuple-element.8, pred[]{:T(512)} %bitcast), kind=kLoop, calls=%fused_computation | loop fusion | flops 6815744 | bytes 2097153 | tf_op jit(solution)/shard_map/jit(_where)/select_n | solution.py:304
  131.2 0.6 slice_reduce_fusion
  (1 shorter events, 0.0 us)
Async XLA Ops:
  3.3 1.2 copy-start

commit v2 on v1

--- a/solution.py
+++ b/solution.py
@@ -14,7 +14,7 @@
 F32 = jnp.float32
 BF16 = jnp.bfloat16
 PIECES = 4
-RELAYED = (2, 3)
+WAYS = ((0, 1, 2, None), (0, 1, 2, None))
 
 
 def mm(a, b):
@@ -63,15 +63,18 @@
         return self.w2 * r + mm(r, self.f)
 
 
-def kernel(n_pairs, n_dates, x_ref, plan_ref, inc_out, stay_out, dis_ref,
-           inc_buf, mov_buf, relay_buf, stay_buf, pan, gram_buf, share, shares,
+def kernel(n_pairs, n_dates, panel_ref, plan_ref, out_ref, dis_ref,
+           x_ref, x_sem, inc_buf, mov_buf, relay_buf, stay_buf, pan, gram_buf, share, shares,
            ring_send, ring_recv, relay_send, relay_recv, fwd_send, gram_send, gram_recv, share_send, share_recv):
-    rows, b2 = x_ref.shape
+    rows, b2 = panel_ref.shape
     b = b2 // 2
     half = b // 2
     height = rows // PIECES
     plane = n_pairs // 4
     p, d = lax.axis_index("pairs"), lax.axis_index("dates")
+    fetch = [pltpu.make_async_copy(panel_ref.at[:, pl.ds(b * k, b)], x_ref.at[:, pl.ds(b * k, b)], x_sem.at[k]) for k in range(2)]
+    for copy in reversed(fetch):
+        copy.start()
     following = lax.rem(p + 1, n_pairs)
 
     barrier = pltpu.get_barrier_semaphore()
@@ -80,17 +83,17 @@
     for k in range(1, n_dates):
         pl.semaphore_signal(barrier, inc=1, device_id=(p, lax.rem(d + k, n_dates)), device_id_type=MESH)
 
+    back = (plane - 1, 3, plane - 4)
     is_corner = lax.rem(p, plane) == plane - 1
-    is_relay = lax.rem(p, plane) == 0
-    relay_at = lax.rem(p - (plane - 1) + n_pairs, n_pairs)
-    relay_to = lax.rem(p + plane, n_pairs)
+    is_relay = [lax.rem(p + k, plane) == plane - 1 for k in back]
+    relay_at = [lax.rem(p - k + n_pairs, n_pairs) for k in back]
+    relay_to = [lax.rem(p + k + 1, n_pairs) for k in back]
 
     eye_half = lax.broadcasted_iota(jnp.int32, (half, half), 0) == lax.broadcasted_iota(jnp.int32, (half, half), 1)
     eye = (lax.broadcasted_iota(jnp.int32, (b, b), 0) == lax.broadcasted_iota(jnp.int32, (b, b), 1)).astype(F32)
     extra_row = lax.broadcasted_iota(jnp.int32, (16, b), 0)
     order = sorted(range(1, n_pairs), key=lambda k: -steps_between(k, n_pairs, 4))
     pieces = [(c, i) for c in range(2) for i in range(PIECES)]
-    relayed = [(c, i) for c in range(2) for i in RELAYED]
 
     def split(v):
         hi = v.astype(BF16).astype(F32)
@@ -98,8 +101,9 @@
 
     previous_slot = None
     for r in range(ROUNDS):
-        slot = plan_ref[r, 0]
+        slot = plan_ref[r]
         if r == 0:
+            fetch[1].wait()
             moves_inc = slot == 0
             inc = [x_ref.at[:, pl.ds(half * c, half)] for c in range(2)]
             stay = x_ref.at[:, pl.ds(b, b)]
@@ -118,6 +122,8 @@
             if r > 0:
                 for i in range(PIECES):
                     incoming[c, i].wait_recv()
+            if r == 0 and c == 0:
+                fetch[0].wait()
             inc_f32 = inc[c][...].astype(F32)
             inc_hi, inc_lo = split(jnp.sum(inc_f32 * inc_f32, axis=0, keepdims=True))
             mine = gram_buf.at[r, c, d]
@@ -132,8 +138,6 @@
                 copy = send(mine, mine, gram_send.at[r, c, k - 1], gram_recv.at[r, c, k - 1], (p, lax.rem(d + k, n_dates)))
                 copy.start()
                 gram_copies.append(copy)
-            if r > 0 and c == 0:
-                forward(1)
         cross = []
         for c in range(2):
             for k in range(n_dates - 1):
@@ -185,19 +189,21 @@
         bottom = ad * mov_side.right_of(d_mov_t)
         rotation = jnp.concatenate([top, bottom], axis=0).astype(BF16)
 
-        landing = inc_out if r == ROUNDS - 1 else inc_buf.at[r]
+        landing = inc_buf.at[r]
         incoming, by_relay, forwards = {}, {}, {}
         for q, (c, i) in enumerate(pieces):
             place = pl.ds(height * i, height)
             incoming[c, i] = send(mov_buf.at[r, c, place], landing.at[c, place], ring_send.at[r, q], ring_recv.at[r, q], (following, d))
-        for q, (c, i) in enumerate(relayed):
-            place = pl.ds(height * i, height)
+            if WAYS[c][i] is None:
+                continue
             way = relay_buf.at[r, q]
-            by_relay[c, i] = send(mov_buf.at[r, c, place], way, relay_send.at[r, q], relay_recv.at[r, q], (relay_at, d))
-            forwards[c, i] = send(way, landing.at[c, place], fwd_send.at[r, q], ring_recv.at[r, c * PIECES + i], (relay_to, d))
+            by_relay[c, i] = send(mov_buf.at[r, c, place], way, relay_send.at[r, q], relay_recv.at[r, q], (relay_at[WAYS[c][i]], d))
+            forwards[c, i] = send(way, landing.at[c, place], fwd_send.at[r, q], ring_recv.at[r, q], (relay_to[WAYS[c][i]], d))
 
         def pass_on(c, i, incoming=incoming, by_relay=by_relay):
-            if i in RELAYED:
+            if WAYS[c][i] is None:
+                incoming[c, i].start()
+            else:
                 @pl.when(is_corner)
                 def _():
                     by_relay[c, i].start()
@@ -205,15 +211,15 @@
                 @pl.when(jnp.logical_not(is_corner))
                 def _():
                     incoming[c, i].start()
-            else:
-                incoming[c, i].start()
-
-        def forward(c, by_relay=by_relay, forwards=forwards):
-            @pl.when(is_relay)
-            def _():
-                for i in RELAYED:
-                    by_relay[c, i].wait_recv()
-                    forwards[c, i].start()
+
+        def forward(by_relay=by_relay, forwards=forwards):
+            for way, here in enumerate(is_relay):
+                @pl.when(here)
+                def _():
+                    for c, i in pieces:
+                        if WAYS[c][i] == way:
+                            by_relay[c, i].wait_recv()
+                            forwards[c, i].start()
 
         for i in range(PIECES):
             place = pl.ds(height * i, height)
@@ -228,20 +234,25 @@
         top = (-ad) * stay_side.right_of(d_mov)
         bottom = a * stay_side.h * eye + a * stay_side.hn
         rotation = jnp.concatenate([top, bottom], axis=0).astype(BF16)
-        target = stay_out if r == ROUNDS - 1 else stay_buf.at[r]
-        target[...] = jnp.dot(pan[...], rotation, preferred_element_type=F32).astype(BF16)
-        forward(0)
+        stay_buf[r] = jnp.dot(pan[...], rotation, preferred_element_type=F32).astype(BF16)
+        forward()
 
         for copy in gram_copies:
             copy.wait_send()
         everyone.wait_send()
         if r == ROUNDS - 1:
-            forward(1)
-            for c, i in pieces:
-                incoming[c, i].wait_recv()
+            for c in range(2):
+                for i in range(PIECES):
+                    incoming[c, i].wait_recv()
+                left, right = pl.ds(half * c, half), pl.ds(b + half * c, half)
+                one, two = inc_buf[r, c], stay_buf[r, :, half * c:half * (c + 1)]
+                out_ref[:, left] = lax.select(slot == 0, one, two)
+                out_ref[:, right] = lax.select(slot == 0, two, one)
         def finish(incoming=incoming, by_relay=by_relay, forwards=forwards):
             for c, i in pieces:
-                if i in RELAYED:
+                if WAYS[c][i] is None:
+                    incoming[c, i].wait_send()
+                else:
                     @pl.when(is_corner)
                     def _():
                         by_relay[c, i].wait_send()
@@ -249,13 +260,10 @@
                     @pl.when(jnp.logical_not(is_corner))
                     def _():
                         incoming[c, i].wait_send()
-                else:
-                    incoming[c, i].wait_send()
-
-            @pl.when(is_relay)
-            def _():
-                for k in relayed:
-                    forwards[k].wait_send()
+
+                    @pl.when(is_relay[WAYS[c][i]])
+                    def _():
+                        forwards[c, i].wait_send()
         finishes = [finish] if r == 0 else finishes + [finish]
     for finish in finishes:
         finish()
@@ -268,40 +276,39 @@
     height = rows // PIECES
     dma = pltpu.SemaphoreType.DMA
     vmem = pl.BlockSpec(memory_space=pltpu.VMEM)
-    moved, stayed, disorder = pl.pallas_call(
+    rotated_panel, disorder = pl.pallas_call(
         functools.partial(kernel, n_pairs, n_dates),
         out_shape=(
-            jax.ShapeDtypeStruct((2, rows, half), BF16),
-            jax.ShapeDtypeStruct((rows, b), BF16),
+            jax.ShapeDtypeStruct((rows, b2), BF16),
             jax.ShapeDtypeStruct((8, 128), F32),
         ),
-        in_specs=[vmem, pl.BlockSpec(memory_space=pltpu.SMEM)],
-        out_specs=(vmem, vmem, vmem),
+        in_specs=[pl.BlockSpec(memory_space=pltpu.HBM), pl.BlockSpec(memory_space=pltpu.SMEM)],
+        out_specs=(vmem, vmem),
         scratch_shapes=[
-            pltpu.VMEM((ROUNDS - 1, 2, rows, half), BF16),
+            pltpu.VMEM((rows, b2), BF16),
+            dma((2,)),
             pltpu.VMEM((ROUNDS, 2, rows, half), BF16),
-            pltpu.VMEM((ROUNDS, 2 * len(RELAYED), height, half), BF16),
-            pltpu.VMEM((ROUNDS - 1, rows, b), BF16),
+            pltpu.VMEM((ROUNDS, 2, rows, half), BF16),
+            pltpu.VMEM((ROUNDS, 2 * PIECES, height, half), BF16),
+            pltpu.VMEM((ROUNDS, rows, b), BF16),
             pltpu.VMEM((rows, b2), BF16),
             pltpu.VMEM((ROUNDS, 2, n_dates, half + 16, b), BF16),
             pltpu.VMEM((ROUNDS, 8, 128), F32),
             pltpu.VMEM((ROUNDS, n_pairs, 128), F32),
             dma((ROUNDS, 2 * PIECES)),
             dma((ROUNDS, 2 * PIECES)),
-            dma((ROUNDS, 2 * len(RELAYED))),
-            dma((ROUNDS, 2 * len(RELAYED))),
-            dma((ROUNDS, 2 * len(RELAYED))),
+            dma((ROUNDS, 2 * PIECES)),
+            dma((ROUNDS, 2 * PIECES)),
+            dma((ROUNDS, 2 * PIECES)),
             dma((ROUNDS, 2, n_dates - 1)),
             dma((ROUNDS, 2, n_dates - 1)),
             dma((ROUNDS,)),
             dma((ROUNDS,)),
         ],
-        compiler_params=pltpu.CompilerParams(collective_id=0, has_side_effects=True, vmem_limit_bytes=48 << 20),
+        compiler_params=pltpu.CompilerParams(collective_id=0, has_side_effects=True, vmem_limit_bytes=62 << 20),
         name="jacobi_rounds",
-    )(returns, plan)
-    front = jnp.concatenate([moved[0], moved[1], stayed], axis=1)
-    back = jnp.concatenate([stayed, moved[0], moved[1]], axis=1)
-    return jnp.where(plan[ROUNDS - 1, 0] == 0, front, back), disorder[:ROUNDS, 0]
+    )(returns, plan.reshape(ROUNDS))
+    return rotated_panel, disorder[:ROUNDS, 0]
 
 
 def solution(mesh):

time: 132 us -> 111 us (0.84)
  Pallas kernels: 125 us -> 106 us
  other arithmetic: 1.35 us -> 0 us
    pallas_call x1, Pallas kernels: 125 us -> 106 us  [local(): pl.pallas_call(functools.partial(kernel, n_pairs, n_dates), out_shape=(ja...]
    select_n x1 -> x0, other arithmetic: 1.35 us -> none  [local(): jnp.where(plan[ROUNDS - 1, 0] == 0, front, back)]
where the time goes in v2:
time: 111 us; the launch traced here: 110 us
  Pallas kernels  106 us (95%)
  local copies, waits for them, and re-layouts  3.56 us (3%)
    pallas_call x1, Pallas kernels, local(): pl.pallas_call(functools.partial(kernel, n_pairs, n_dates), out_shape=(ja...  106 us
    unnamed x1, local copies, waits for them, and re-layouts  2.26 us

profile of v2, /device:TPU:32, one launch (start us, length us, event | category | flops | bytes accessed | tf_op | source)
XLA Modules:
  0.0 110.4 jit_solution(1738161706191436971)
XLA Ops:
  0.6 106.2 %jacobi_rounds.1 = (bf16[1024,512]{1,0:T(8,128)(2,1)}, f32[8,128]{1,0:T(8,128)}) custom-call(bf16[1024,512]{1,0:T(8,128)(2,1)} %panel_ref.1, s32[3]{0:T(128)} %bitcast.1), custom_call_target="tpu_custom_call" | custom-call | tf_op jit(solution)/shard_map/jacobi_rounds/pallas_call | solution.py:279
  106.9 1.3 %slice_reduce_fusion = f32[3]{0:T(128)} fusion(f32[8,128]{1,0:T(8,128)} %get-tuple-element.5), kind=kLoop, calls=%fused_computation | loop fusion | bytes 24 | tf_op jit(solution)/shard_map/slice | solution.py:311
  108.2 2.3 %copy.5 = bf16[1024,512]{1,0:T(8,128)(2,1)} copy(bf16[1024,512]{1,0:T(8,128)(2,1)} %get-tuple-element.8) | data formatting | bytes 2097152

commit v3 on v2

--- a/solution.py
+++ b/solution.py
@@ -13,8 +13,9 @@
 MESH = pl.DeviceIdType.MESH
 F32 = jnp.float32
 BF16 = jnp.bfloat16
-PIECES = 4
-WAYS = ((0, 1, 2, None), (0, 1, 2, None))
+PIECES = 8
+STRAIGHT = None
+WAYS = ((2,0,1,STRAIGHT,2,0,1,STRAIGHT),(2,0,1,STRAIGHT,2,STRAIGHT,STRAIGHT,STRAIGHT))
 
 
 def mm(a, b):
@@ -31,10 +32,16 @@
     )
 
 
-def steps_between(k, n_pairs, row):
-    x, y, z = k % row, (k // row) % row, k // (row * row)
-    depth = n_pairs // (row * row)
-    return min(x, row - x) + min(y, row - y) + 2 * min(z, depth - z)
+def chip_steps(n_pairs):
+    depth = n_pairs // 16
+    places = [(dz, dy, dx) for dz in range(depth) for dy in range(4) for dx in range(4) if (dz, dy, dx) != (0, 0, 0)]
+
+    def chips(place):
+        dz, dy, dx = place
+        along_z = 2 * min(dz, depth - dz) - (2 * dz == depth)
+        return along_z + min(dy, 4 - dy) + min(dx, 4 - dx)
+
+    return sorted(places, key=chips, reverse=True)
 
 
 class Side:
@@ -77,9 +84,16 @@
         copy.start()
     following = lax.rem(p + 1, n_pairs)
 
+    depth = n_pairs // 16
+    pz, py, px = p // 16, lax.rem(p // 4, 4), lax.rem(p, 4)
+    partners = []
+    for dz, dy, dx in chip_steps(n_pairs):
+        pair = lax.rem(pz + dz, depth) * 16 + lax.rem(py + dy, 4) * 4 + lax.rem(px + dx, 4)
+        partners.append((pair, lax.rem(d + n_dates // 2, n_dates) if 2 * dz == depth else d))
+
     barrier = pltpu.get_barrier_semaphore()
-    for k in range(1, n_pairs):
-        pl.semaphore_signal(barrier, inc=1, device_id=(lax.rem(p + k, n_pairs), d), device_id_type=MESH)
+    for partner in partners:
+        pl.semaphore_signal(barrier, inc=1, device_id=partner, device_id_type=MESH)
     for k in range(1, n_dates):
         pl.semaphore_signal(barrier, inc=1, device_id=(p, lax.rem(d + k, n_dates)), device_id_type=MESH)
 
@@ -92,7 +106,6 @@
     eye_half = lax.broadcasted_iota(jnp.int32, (half, half), 0) == lax.broadcasted_iota(jnp.int32, (half, half), 1)
     eye = (lax.broadcasted_iota(jnp.int32, (b, b), 0) == lax.broadcasted_iota(jnp.int32, (b, b), 1)).astype(F32)
     extra_row = lax.broadcasted_iota(jnp.int32, (16, b), 0)
-    order = sorted(range(1, n_pairs), key=lambda k: -steps_between(k, n_pairs, 4))
     pieces = [(c, i) for c in range(2) for i in range(PIECES)]
 
     def split(v):
@@ -134,7 +147,7 @@
             mine[half:half + 16, :] = extra.astype(BF16)
             if r == 0 and c == 0:
                 pl.semaphore_wait(barrier, n_pairs - 1 + n_dates - 1)
-            for k in range(1, n_dates):
+            for k in (2, 1, 3):
                 copy = send(mine, mine, gram_send.at[r, c, k - 1], gram_recv.at[r, c, k - 1], (p, lax.rem(d + k, n_dates)))
                 copy.start()
                 gram_copies.append(copy)
@@ -156,9 +169,8 @@
         share[r] = mine
         shares[r, pl.ds(p, 1), :] = mine[0:1]
         share_copies = []
-        for k in order:
-            copy = send(share.at[r, pl.ds(0, 1)], shares.at[r, pl.ds(p, 1)], share_send.at[r], share_recv.at[r],
-                        (lax.rem(p + k, n_pairs), d))
+        for partner in partners:
+            copy = send(share.at[r, pl.ds(0, 1)], shares.at[r, pl.ds(p, 1)], share_send.at[r], share_recv.at[r], partner)
             copy.start()
             share_copies.append(copy)
 
@@ -305,7 +317,7 @@
             dma((ROUNDS,)),
             dma((ROUNDS,)),
         ],
-        compiler_params=pltpu.CompilerParams(collective_id=0, has_side_effects=True, vmem_limit_bytes=62 << 20),
+        compiler_params=pltpu.CompilerParams(collective_id=0, has_side_effects=True, vmem_limit_bytes=52 << 20),
         name="jacobi_rounds",
     )(returns, plan.reshape(ROUNDS))
     return rotated_panel, disorder[:ROUNDS, 0]

time: 111 us -> 105 us (0.946); the launches traced: 110 us -> 103 us
  Pallas kernels: 106 us -> 100 us
  local copies, waits for them, and re-layouts: 3.56 us -> 2.24 us
    pallas_call x1, Pallas kernels: 106 us -> 100 us  [local(): pl.pallas_call(functools.partial(kernel, n_pairs, n_dates), out_shape=(ja...]
    unnamed x1 -> x3, local copies, waits for them, and re-layouts: 2.26 us -> 1.62 us
where the time goes in v3:
time: 105 us; the launch traced here: 103 us
  Pallas kernels  100 us (95%)
  local copies, waits for them, and re-layouts  2.24 us (2%)
    pallas_call x1, Pallas kernels, local(): pl.pallas_call(functools.partial(kernel, n_pairs, n_dates), out_shape=(ja...  100 us

profile of v3, /device:TPU:32, one launch (start us, length us, event | category | flops | bytes accessed | tf_op | source)
XLA Modules:
  0.0 103.1 jit_solution(6347270570955798226)
XLA Ops:
  0.6 0.0 copy-start
  0.6 0.6 copy-done
  1.3 100.2 %jacobi_rounds.1 = (bf16[1024,512]{1,0:T(8,128)(2,1)S(1)}, f32[8,128]{1,0:T(8,128)S(1)}) custom-call(bf16[1024,512]{1,0:T(8,128)(2,1)} %panel_ref.1, s32[3]{0:T(128)S(1)} %bitcast.1), custom_call_target="tpu_custom_call" | custom-call | tf_op jit(solution)/shard_map/jacobi_rounds/pallas_call | solution.py:291
  101.5 0.6 slice_reduce_fusion
  102.1 1.0 copy.5
Async XLA Ops:
  0.6 0.7 copy-start

commit v4 on v3

--- a/solution.py
+++ b/solution.py
@@ -15,7 +15,10 @@
 BF16 = jnp.bfloat16
 PIECES = 8
 STRAIGHT = None
-WAYS = ((2,0,1,STRAIGHT,2,0,1,STRAIGHT),(2,0,1,STRAIGHT,2,STRAIGHT,STRAIGHT,STRAIGHT))
+WAYS = (
+    (2, 0, 1, 2, 0, 1, STRAIGHT, STRAIGHT),
+    (2, 0, 1, STRAIGHT, STRAIGHT, STRAIGHT, STRAIGHT, STRAIGHT),
+)
 
 
 def mm(a, b):
@@ -147,8 +150,8 @@
             mine[half:half + 16, :] = extra.astype(BF16)
             if r == 0 and c == 0:
                 pl.semaphore_wait(barrier, n_pairs - 1 + n_dates - 1)
-            for k in (2, 1, 3):
-                copy = send(mine, mine, gram_send.at[r, c, k - 1], gram_recv.at[r, c, k - 1], (p, lax.rem(d + k, n_dates)))
+            for k in (2, 3, 1):
+                copy = send(mine, mine, gram_send.at[r, c, k - 1], gram_recv.at[r, c, k - 1], (p, jnp.bitwise_xor(d, k)))
                 copy.start()
                 gram_copies.append(copy)
         cross = []

time: 105 us -> 105 us (level)
  no operation moved by 1% of the time
where the time goes in v4:
time: 105 us; the launch traced here: 104 us
  Pallas kernels  101 us (96%)
  local copies, waits for them, and re-layouts  2.24 us (2%)
    pallas_call x1, Pallas kernels, local(): pl.pallas_call(functools.partial(kernel, n_pairs, n_dates), out_shape=(ja...  101 us

profile of v4, /device:TPU:32, one launch (start us, length us, event | category | flops | bytes accessed | tf_op | source)
XLA Modules:
  0.0 104.0 jit_solution(689887825960835396)
XLA Ops:
  0.6 0.0 copy-start
  0.6 0.6 copy-done
  1.3 101.1 %jacobi_rounds.1 = (bf16[1024,512]{1,0:T(8,128)(2,1)S(1)}, f32[8,128]{1,0:T(8,128)S(1)}) custom-call(bf16[1024,512]{1,0:T(8,128)(2,1)} %panel_ref.1, s32[3]{0:T(128)S(1)} %bitcast.1), custom_call_target="tpu_custom_call" | custom-call | tf_op jit(solution)/shard_map/jacobi_rounds/pallas_call | solution.py:294
  102.4 0.6 slice_reduce_fusion
  103.0 1.0 copy.5
Async XLA Ops:
  0.6 0.7 copy-start

commit v5 on v4

--- a/solution.py
+++ b/solution.py
@@ -133,7 +133,7 @@
         stay_f32 = stay[...].astype(F32)
         stay_sq = jnp.sum(stay_f32 * stay_f32, axis=0, keepdims=True)
         stay_hi, stay_lo = split(stay_sq)
-        gram_copies = []
+        gram_copies, arrivals = [], ([], [])
         for c in range(2):
             if r > 0:
                 for i in range(PIECES):
@@ -150,14 +150,23 @@
             mine[half:half + 16, :] = extra.astype(BF16)
             if r == 0 and c == 0:
                 pl.semaphore_wait(barrier, n_pairs - 1 + n_dates - 1)
-            for k in (2, 3, 1):
+            for k in (2, 1) if r == 0 else (2, 3, 1):
                 copy = send(mine, mine, gram_send.at[r, c, k - 1], gram_recv.at[r, c, k - 1], (p, jnp.bitwise_xor(d, k)))
                 copy.start()
                 gram_copies.append(copy)
+                arrivals[c].append(copy)
+        if r == 0:
+            for c in range(2):
+                arrivals[c].pop(0).wait_recv()
+                other = gram_buf.at[r, c, jnp.bitwise_xor(d, 2)]
+                copy = send(other, other, gram_send.at[r, c, 2], gram_recv.at[r, c, 2], (p, jnp.bitwise_xor(d, 1)))
+                copy.start()
+                gram_copies.append(copy)
+                arrivals[c].append(copy)
         cross = []
         for c in range(2):
-            for k in range(n_dates - 1):
-                gram_copies[c * (n_dates - 1) + k].wait_recv()
+            for copy in arrivals[c]:
+                copy.wait_recv()
             total = gram_buf[r, c, 0].astype(F32)
             for k in range(1, n_dates):
                 total = total + gram_buf[r, c, k].astype(F32)

time: 105 us -> 103 us (0.981)
  Pallas kernels: 101 us -> 98.9 us
    pallas_call x1, Pallas kernels: 101 us -> 98.9 us  [local(): pl.pallas_call(functools.partial(kernel, n_pairs, n_dates), out_shape=(ja...]
where the time goes in v5:
time: 103 us; the launch traced here: 102 us
  Pallas kernels  98.9 us (96%)
  local copies, waits for them, and re-layouts  2.24 us (2%)
    pallas_call x1, Pallas kernels, local(): pl.pallas_call(functools.partial(kernel, n_pairs, n_dates), out_shape=(ja...  98.9 us

profile of v5, /device:TPU:32, one launch (start us, length us, event | category | flops | bytes accessed | tf_op | source)
XLA Modules:
  0.0 101.8 jit_solution(12333176083161702114)
XLA Ops:
  0.6 0.0 copy-start
  0.6 0.6 copy-done
  1.3 98.9 %jacobi_rounds.1 = (bf16[1024,512]{1,0:T(8,128)(2,1)S(1)}, f32[8,128]{1,0:T(8,128)S(1)}) custom-call(bf16[1024,512]{1,0:T(8,128)(2,1)} %panel_ref.1, s32[3]{0:T(128)S(1)} %bitcast.1), custom_call_target="tpu_custom_call" | custom-call | tf_op jit(solution)/shard_map/jacobi_rounds/pallas_call | solution.py:303
  100.2 0.6 slice_reduce_fusion
  100.8 1.0 copy.5
Async XLA Ops:
  0.6 0.7 copy-start
